TPU v7x, 32 devices: a whole 2x2x4 slice. The times are simulated.
32 devices in a mesh: row: 8 (over z, x), col: 4 (over y, core).
Axes of the slice: x: 2, y: 2, z: 4, core: 2. Of those that a mesh axis runs over, the one named last changes fastest.
Arguments:
- panel_transposed: float32 [256, 16384], P('col', 'row'), may hold values from -0.046875 to 0.046875
- trailing: float32 [16384, 2048], P('row', 'col'), may hold values from -6 to 6
Outputs:
- stop_factors: float32 [2048, 256], P('row')
- stop_blocks: float32 [2048, 2048], P('row', 'col')
- projected: float32 [16384, 2048], P('row', 'col')
All inputs are finite; a program needn't handle non-finite values.
Results may differ from a plain program's by a relative error of at most 0.00026.
Values sent between devices are 32-bit elements; how exact they have to be, the bound alone decides.
A program may use at most 128 MiB of HBM per device.

v0:
```python
import jax
import jax.numpy as jnp
from jax import lax
from jax.sharding import PartitionSpec as P


def prefix(part, axis, combine, identity):
    place = lax.axis_index(axis)
    gathered = lax.all_gather(part, axis)
    state = jnp.zeros_like(part) + jnp.asarray(identity, part.dtype)

    def one(turn, state):
        return combine(state, lax.dynamic_index_in_dim(gathered, turn, 0, False))

    return lax.fori_loop(0, place, one, state)


def spread(block, axis, owner):
    block = jnp.where(lax.axis_index(axis) == owner, block, jnp.zeros_like(block))
    return lax.psum(block, axis)


def add_pair(earlier, later):
    return earlier + later


def matmul(left, right):
    return jnp.dot(left, right, precision=lax.Precision.HIGHEST, preferred_element_type=jnp.float32)


def factor_inverse(matrix):
    order = matrix.shape[0]
    if order == 1:
        lower = jnp.sqrt(matrix)
        return (lower, 1.0 / lower)
    half = order // 2
    lower_top, inverse_top = factor_inverse(matrix[:half, :half])
    lower_side = matmul(matrix[half:, :half], inverse_top.T)
    schur = matrix[half:, half:] - matmul(lower_side, lower_side.T)
    lower_bottom, inverse_bottom = factor_inverse(schur)
    inverse_side = -matmul(matmul(inverse_bottom, lower_side), inverse_top)
    upper_zeros = jnp.zeros((half, order - half), jnp.float32)
    lower = jnp.concatenate(
        [
            jnp.concatenate([lower_top, upper_zeros], 1),
            jnp.concatenate([lower_side, lower_bottom], 1),
        ],
        0,
    )
    inverse = jnp.concatenate(
        [
            jnp.concatenate([inverse_top, upper_zeros], 1),
            jnp.concatenate([inverse_side, inverse_bottom], 1),
        ],
        0,
    )
    return (lower, inverse)


def factor_sums(sums, width):
    lower, inverse = factor_inverse(sums[:, :width])
    blocks = matmul(inverse, sums[:, width:])
    return (lower.T, inverse, blocks)


def shards(panel_transposed, trailing):
    highest = lax.Precision.HIGHEST
    whole = lax.all_gather(panel_transposed, "col", axis=0, tiled=True)
    width = whole.shape[0]
    own_gram = lax.dot_general(
        whole,
        whole,
        (((1,), (1,)), ((), ())),
        precision=highest,
        preferred_element_type=jnp.float32,
    )
    own_cross = jnp.dot(whole, trailing, precision=highest, preferred_element_type=jnp.float32)
    own_both = jnp.concatenate([own_gram, own_cross], 1)
    earlier = prefix(own_both, "row", add_pair, jnp.zeros_like(own_both))
    prefix_sums = earlier + own_both
    stop_factors, stop_inverse, stop_blocks = factor_sums(prefix_sums, width)
    final = spread(jnp.concatenate([stop_inverse, stop_blocks], 1), "row", lax.axis_size("row") - 1)
    final_inverse = final[:, :width]
    final_blocks = final[:, width:]
    coeffs = matmul(final_inverse.T, final_blocks)
    removed = lax.dot_general(
        whole,
        coeffs,
        (((0,), (0,)), ((), ())),
        precision=highest,
        preferred_element_type=jnp.float32,
    )
    projected = trailing - removed
    return (stop_factors, stop_blocks, projected)


def solution(mesh):
    return jax.shard_map(
        shards,
        mesh=mesh,
        in_specs=(P("col", "row"), P("row", "col")),
        out_specs=(P("row", None), P("row", "col"), P("row", "col")),
        check_vma=False,
    )
```

profile of v0, /device:TPU:0, one launch (start us, length us, event | category | flops | bytes accessed | tf_op | source)
XLA Modules:
  0.0 713.9 jit_solution(4968217151157308787)
XLA Ops:
  7.9 26.9 %all-gather.4.cloned.1.call-done = f32[256,2048]{1,0:T(8,128)} async-done(((f32[64,2048]{1,0:T(8,128)}), f32[256,2048]{1,0:T(8,128)}) %all-gather.4.cloned.1.call-update) | async-done | bytes 2097168 | tf_op jit(solution)/shard_map/all_gather | solution.py:68
  34.9 4.2 fusion.2455
  39.1 5.7 fusion.2456
  44.9 0.9 pad_maximum_fusion
  45.9 5.3 copy.135
  51.2 93.8 %all-gather.6.cloned.1.call-done = f32[2048,768]{1,0:T(8,128)} async-done(((f32[256,768]{1,0:T(8,128)}), f32[2048,768]{1,0:T(8,128)}) %all-gather.6.cloned.1.call-update) | async-done | bytes 6291472 | tf_op jit(solution)/shard_map/all_gather | solution.py:9
  145.3 1.0 fusion.2326
  146.3 0.9 copy-done.2
  150.0 0.8 fusion.1972
  154.8 0.8 fusion.1524
  163.1 0.8 fusion.1010
  178.4 0.8 fusion.622
  179.3 0.8 convolution_subtract_fusion.14
  207.7 0.9 fusion.368
  208.6 0.9 convolution_subtract_fusion.6
  264.6 0.9 fusion.208
  265.5 0.9 convolution_subtract_fusion.2
  592.9 0.8 convolution_subtract_fusion.63
  596.6 0.9 fusion.2070
  597.5 0.8 convolution_negate_fusion.63
  598.3 0.9 fusion.1492
  599.1 0.8 convolution_negate_fusion.31
  600.0 0.9 fusion.978
  600.9 0.8 convolution_negate_fusion.15
  601.7 0.9 fusion.606
  602.7 0.9 fusion.360
  604.1 0.9 fusion.204
  605.3 1.0 fusion.106
  606.7 1.4 fusion.2
  608.1 0.8 copy-done.4
  608.9 1.8 maximum_select_fusion
  617.4 0.8 fusion.1254
  626.8 0.8 fusion.1155
  627.5 0.8 fusion.712
  628.3 0.8 fusion.430
  629.1 0.8 fusion.1199
  629.9 0.8 fusion.746
  630.7 0.8 fusion.453
  631.4 0.8 fusion.1243
  633.0 0.8 fusion.476
  634.5 0.8 fusion.814
  635.3 0.8 fusion.499
  636.0 0.8 fusion.1331
  636.8 0.8 fusion.848
  637.6 0.8 fusion.522
  639.1 0.8 fusion.882
  639.9 0.8 fusion.545
  640.7 0.8 fusion.1419
  641.5 0.8 fusion.916
  642.3 0.8 fusion.568
  643.0 0.8 fusion.1463
  644.6 0.8 fusion.283
  645.3 0.8 fusion.950
  646.1 0.8 fusion.591
  647.7 0.8 fusion.341
  648.4 0.8 fusion.146
  649.2 0.8 fusion.181
  650.0 0.8 fusion.79
  650.8 0.8 fusion.60
  651.6 0.8 copy.136
  652.4 40.6 %all-reduce.256.cloned.1.call-done = f32[256,768]{1,0:T(8,128)} async-done(((f32[256,768]{1,0:T(8,128)}), f32[256,768]{1,0:T(8,128)}) %all-reduce.256.cloned.1.call-update) | async-done | bytes 786448 | tf_op jit(solution)/shard_map/psum | solution.py:20
  693.0 1.8 fusion
  694.8 6.8 bitcast_subtract_fusion
  701.6 5.3 copy.137
  (1174 shorter events, 192.5 us)
Async XLA Ops:
  7.2 27.7 %all-gather.4.cloned.1.call-start = ((), (), s32[]{:S(2)}) async-start(), calls=%async_computation | async-start | bytes 2621440 | tf_op jit(solution)/shard_map/all_gather | solution.py:68
  7.9 137.1 %all-gather.6.cloned.1.call-start = ((), (), s32[]{:S(2)}) async-start(), calls=%async_computation.2 | async-start | bytes 7077888 | tf_op jit(solution)/shard_map/all_gather | solution.py:9
  45.8 647.2 %all-reduce.256.cloned.1.call-start = ((), (), s32[]{:S(2)}) async-start(), calls=%async_computation.1 | async-start | bytes 1572864 | tf_op jit(solution)/shard_map/psum | solution.py:20
  147.8 227.8 %copy-start.3 = (f32[256,768]{1,0:T(8,128)S(1)}, f32[256,768]{1,0:T(8,128)}, u32[]{:S(2)}) copy-start(f32[256,768]{1,0:T(8,128)} %copy-done.2) | copy-start | bytes 2359300
  155.6 7.6 %copy-start.22 = (f32[4,4]{1,0:T(4,128)}, f32[4,4]{1,0:T(4,128)S(1)}, u32[]{:S(2)}) copy-start(f32[4,4]{1,0:T(4,128)S(1)} %fusion.1524) | copy-start | bytes 196
  159.4 11.7 %copy-start.114 = (f32[2,2]{1,0:T(2,128)}, f32[2,2]{1,0:T(2,128)S(1)}, u32[]{:S(2)}) copy-start(f32[2,2]{1,0:T(2,128)S(1)} %fusion.2068) | copy-start | bytes 52
  163.9 14.5 %copy-start.5 = (f32[8,8]{1,0:T(8,128)}, f32[8,8]{1,0:T(8,128)S(1)}, u32[]{:S(2)}) copy-start(f32[8,8]{1,0:T(8,128)S(1)} %fusion.1010) | copy-start | bytes 772
  174.4 15.0 %copy-start.115 = (f32[2,2]{1,0:T(2,128)}, f32[2,2]{1,0:T(2,128)S(1)}, u32[]{:S(2)}) copy-start(f32[2,2]{1,0:T(2,128)S(1)} %fusion.2064) | copy-start | bytes 52
  189.5 46.3 %copy-start.117 = (f32[2,2]{1,0:T(2,128)}, f32[2,2]{1,0:T(2,128)S(1)}, u32[]{:S(2)}) copy-start(f32[2,2]{1,0:T(2,128)S(1)} %fusion.2062) | copy-start | bytes 52
  200.1 7.4 %copy-start.26 = (f32[4,4]{1,0:T(4,128)}, f32[4,4]{1,0:T(4,128)S(1)}, u32[]{:S(2)}) copy-start(f32[4,4]{1,0:T(4,128)S(1)} %fusion.1746) | copy-start | bytes 196
  222.9 70.0 %copy-start.6 = (f32[8,8]{1,0:T(8,128)}, f32[8,8]{1,0:T(8,128)S(1)}, u32[]{:S(2)}) copy-start(f32[8,8]{1,0:T(8,128)S(1)} %fusion.1006) | copy-start | bytes 772
  229.4 145.2 %copy-start.34 = (f32[4,4]{1,0:T(4,128)}, f32[4,4]{1,0:T(4,128)S(1)}, u32[]{:S(2)}) copy-start(f32[4,4]{1,0:T(4,128)S(1)} %fusion.1744) | copy-start | bytes 196
  243.3 49.7 %copy-start.36 = (f32[4,4]{1,0:T(4,128)}, f32[4,4]{1,0:T(4,128)S(1)}, u32[]{:S(2)}) copy-start(f32[4,4]{1,0:T(4,128)S(1)} %fusion.1518) | copy-start | bytes 196
  246.4 17.2 %copy-start.120 = (f32[2,2]{1,0:T(2,128)}, f32[2,2]{1,0:T(2,128)S(1)}, u32[]{:S(2)}) copy-start(f32[2,2]{1,0:T(2,128)S(1)} %fusion.2050) | copy-start | bytes 52
  279.4 13.6 %copy-start.7 = (f32[8,8]{1,0:T(8,128)}, f32[8,8]{1,0:T(8,128)S(1)}, u32[]{:S(2)}) copy-start(f32[8,8]{1,0:T(8,128)S(1)} %fusion.1002) | copy-start | bytes 772
  302.6 40.7 %copy-start.124 = (f32[2,2]{1,0:T(2,128)}, f32[2,2]{1,0:T(2,128)S(1)}, u32[]{:S(2)}) copy-start(f32[2,2]{1,0:T(2,128)S(1)} %fusion.2038) | copy-start | bytes 52
  330.4 12.8 %copy-start.125 = (f32[2,2]{1,0:T(2,128)}, f32[2,2]{1,0:T(2,128)S(1)}, u32[]{:S(2)}) copy-start(f32[2,2]{1,0:T(2,128)S(1)} %fusion.2032) | copy-start | bytes 52
  334.1 13.3 %copy-start.8 = (f32[8,8]{1,0:T(8,128)}, f32[8,8]{1,0:T(8,128)S(1)}, u32[]{:S(2)}) copy-start(f32[8,8]{1,0:T(8,128)S(1)} %fusion.998) | copy-start | bytes 772
  340.4 20.1 %copy-start.48 = (f32[4,4]{1,0:T(4,128)}, f32[4,4]{1,0:T(4,128)S(1)}, u32[]{:S(2)}) copy-start(f32[4,4]{1,0:T(4,128)S(1)} %fusion.1736) | copy-start | bytes 196
  357.1 17.4 %copy-start.127 = (f32[2,2]{1,0:T(2,128)}, f32[2,2]{1,0:T(2,128)S(1)}, u32[]{:S(2)}) copy-start(f32[2,2]{1,0:T(2,128)S(1)} %fusion.2026) | copy-start | bytes 52
  367.4 7.9 %copy-start.17 = (f32[4,4]{1,0:T(4,128)}, f32[4,4]{1,0:T(4,128)S(1)}, u32[]{:S(2)}) copy-start(f32[4,4]{1,0:T(4,128)S(1)} %fusion.1734) | copy-start | bytes 196
  385.7 13.6 %copy-start.128 = (f32[2,2]{1,0:T(2,128)}, f32[2,2]{1,0:T(2,128)S(1)}, u32[]{:S(2)}) copy-start(f32[2,2]{1,0:T(2,128)S(1)} %fusion.2020) | copy-start | bytes 52
  389.6 68.4 %copy-start.9 = (f32[8,8]{1,0:T(8,128)}, f32[8,8]{1,0:T(8,128)S(1)}, u32[]{:S(2)}) copy-start(f32[8,8]{1,0:T(8,128)S(1)} %fusion.994) | copy-start | bytes 772
  413.1 17.1 %copy-start.131 = (f32[2,2]{1,0:T(2,128)}, f32[2,2]{1,0:T(2,128)S(1)}, u32[]{:S(2)}) copy-start(f32[2,2]{1,0:T(2,128)S(1)} %fusion.2014) | copy-start | bytes 52
  444.4 68.1 %copy-start.10 = (f32[8,8]{1,0:T(8,128)}, f32[8,8]{1,0:T(8,128)S(1)}, u32[]{:S(2)}) copy-start(f32[8,8]{1,0:T(8,128)S(1)} %fusion.990) | copy-start | bytes 772
  450.9 26.3 %copy-start.62 = (f32[4,4]{1,0:T(4,128)}, f32[4,4]{1,0:T(4,128)S(1)}, u32[]{:S(2)}) copy-start(f32[4,4]{1,0:T(4,128)S(1)} %fusion.1728) | copy-start | bytes 196
  467.6 9.7 %copy-start.134 = (f32[2,2]{1,0:T(2,128)}, f32[2,2]{1,0:T(2,128)S(1)}, u32[]{:S(2)}) copy-start(f32[2,2]{1,0:T(2,128)S(1)} %fusion.2002) | copy-start | bytes 52
  474.2 10.5 %copy-start.88 = (f32[2,2]{1,0:T(2,128)}, f32[2,2]{1,0:T(2,128)S(1)}, u32[]{:S(2)}) copy-start(f32[2,2]{1,0:T(2,128)S(1)} %fusion.2000) | copy-start | bytes 52
  498.9 13.5 %copy-start.11 = (f32[8,8]{1,0:T(8,128)}, f32[8,8]{1,0:T(8,128)S(1)}, u32[]{:S(2)}) copy-start(f32[8,8]{1,0:T(8,128)S(1)} %fusion.986) | copy-start | bytes 772
  505.4 20.5 %copy-start.70 = (f32[4,4]{1,0:T(4,128)}, f32[4,4]{1,0:T(4,128)S(1)}, u32[]{:S(2)}) copy-start(f32[4,4]{1,0:T(4,128)S(1)} %fusion.1724) | copy-start | bytes 196
  522.3 13.4 %copy-start.137 = (f32[2,2]{1,0:T(2,128)}, f32[2,2]{1,0:T(2,128)S(1)}, u32[]{:S(2)}) copy-start(f32[2,2]{1,0:T(2,128)S(1)} %fusion.1990) | copy-start | bytes 52
  553.6 26.6 %copy-start.12 = (f32[8,8]{1,0:T(8,128)}, f32[8,8]{1,0:T(8,128)S(1)}, u32[]{:S(2)}) copy-start(f32[8,8]{1,0:T(8,128)S(1)} %fusion.982) | copy-start | bytes 772
  576.6 16.2 %copy-start.141 = (f32[2,2]{1,0:T(2,128)}, f32[2,2]{1,0:T(2,128)S(1)}, u32[]{:S(2)}) copy-start(f32[2,2]{1,0:T(2,128)S(1)} %fusion.1978) | copy-start | bytes 52
  580.3 12.4 %copy-start.15 = (f32[8,8]{1,0:T(8,128)}, f32[8,8]{1,0:T(8,128)S(1)}, u32[]{:S(2)}) copy-start(f32[8,8]{1,0:T(8,128)S(1)} %fusion.972) | copy-start | bytes 772
  592.8 11.3 %copy-start.16 = (f32[16,32]{1,0:T(8,128)}, f32[16,32]{1,0:T(8,128)S(1)}, u32[]{:S(2)}) copy-start(f32[16,32]{1,0:T(8,128)S(1)} %concatenate.6106) | copy-start | bytes 6148
  592.8 11.2 %copy-start.14 = (f32[32,64]{1,0:T(8,128)}, f32[32,64]{1,0:T(8,128)S(1)}, u32[]{:S(2)}) copy-start(f32[32,64]{1,0:T(8,128)S(1)} %concatenate.6105) | copy-start | bytes 24580
  604.0 23.5 %copy-start.23 = (f32[4,4]{1,0:T(4,128)S(1)}, f32[4,4]{1,0:T(4,128)}, u32[]{:S(2)}) copy-start(f32[4,4]{1,0:T(4,128)} %copy-done.22) | copy-start | bytes 196
  604.0 23.5 %copy-start.29 = (f32[4,4]{1,0:T(4,128)S(1)}, f32[4,4]{1,0:T(4,128)}, u32[]{:S(2)}) copy-start(f32[4,4]{1,0:T(4,128)} %copy-done.28) | copy-start | bytes 196
  604.1 42.1 %copy-start.13 = (f32[8,8]{1,0:T(8,128)S(1)}, f32[8,8]{1,0:T(8,128)}, u32[]{:S(2)}) copy-start(f32[8,8]{1,0:T(8,128)} %copy-done.12) | copy-start | bytes 772
  604.1 45.9 %copy-start.18 = (f32[4,4]{1,0:T(4,128)S(1)}, f32[4,4]{1,0:T(4,128)}, u32[]{:S(2)}) copy-start(f32[4,4]{1,0:T(4,128)} %copy-done.17) | copy-start | bytes 196
  605.2 23.1 %copy-start.25 = (f32[4,4]{1,0:T(4,128)S(1)}, f32[4,4]{1,0:T(4,128)}, u32[]{:S(2)}) copy-start(f32[4,4]{1,0:T(4,128)} %copy-done.24) | copy-start | bytes 196
  605.2 24.7 %copy-start.31 = (f32[4,4]{1,0:T(4,128)S(1)}, f32[4,4]{1,0:T(4,128)}, u32[]{:S(2)}) copy-start(f32[4,4]{1,0:T(4,128)} %copy-done.30) | copy-start | bytes 196
  605.2 24.7 %copy-start.37 = (f32[4,4]{1,0:T(4,128)S(1)}, f32[4,4]{1,0:T(4,128)}, u32[]{:S(2)}) copy-start(f32[4,4]{1,0:T(4,128)} %copy-done.36) | copy-start | bytes 196
  605.2 25.4 %copy-start.35 = (f32[4,4]{1,0:T(4,128)S(1)}, f32[4,4]{1,0:T(4,128)}, u32[]{:S(2)}) copy-start(f32[4,4]{1,0:T(4,128)} %copy-done.34) | copy-start | bytes 196
  605.2 27.0 %copy-start.39 = (f32[4,4]{1,0:T(4,128)S(1)}, f32[4,4]{1,0:T(4,128)}, u32[]{:S(2)}) copy-start(f32[4,4]{1,0:T(4,128)} %copy-done.38) | copy-start | bytes 196
  605.2 27.7 %copy-start.41 = (f32[4,4]{1,0:T(4,128)S(1)}, f32[4,4]{1,0:T(4,128)}, u32[]{:S(2)}) copy-start(f32[4,4]{1,0:T(4,128)} %copy-done.40) | copy-start | bytes 196
  605.2 38.6 %copy-start.27 = (f32[4,4]{1,0:T(4,128)S(1)}, f32[4,4]{1,0:T(4,128)}, u32[]{:S(2)}) copy-start(f32[4,4]{1,0:T(4,128)} %copy-done.26) | copy-start | bytes 196
  605.2 43.2 %copy-start.33 = (f32[4,4]{1,0:T(4,128)S(1)}, f32[4,4]{1,0:T(4,128)}, u32[]{:S(2)}) copy-start(f32[4,4]{1,0:T(4,128)} %copy-done.32) | copy-start | bytes 196
  606.5 25.7 %copy-start.45 = (f32[4,4]{1,0:T(4,128)S(1)}, f32[4,4]{1,0:T(4,128)}, u32[]{:S(2)}) copy-start(f32[4,4]{1,0:T(4,128)} %copy-done.44) | copy-start | bytes 196
  606.5 28.0 %copy-start.47 = (f32[4,4]{1,0:T(4,128)S(1)}, f32[4,4]{1,0:T(4,128)}, u32[]{:S(2)}) copy-start(f32[4,4]{1,0:T(4,128)} %copy-done.46) | copy-start | bytes 196
  606.5 28.0 %copy-start.51 = (f32[4,4]{1,0:T(4,128)S(1)}, f32[4,4]{1,0:T(4,128)}, u32[]{:S(2)}) copy-start(f32[4,4]{1,0:T(4,128)} %copy-done.50) | copy-start | bytes 196
  606.5 28.7 %copy-start.49 = (f32[4,4]{1,0:T(4,128)S(1)}, f32[4,4]{1,0:T(4,128)}, u32[]{:S(2)}) copy-start(f32[4,4]{1,0:T(4,128)} %copy-done.48) | copy-start | bytes 196
  606.6 30.3 %copy-start.53 = (f32[4,4]{1,0:T(4,128)S(1)}, f32[4,4]{1,0:T(4,128)}, u32[]{:S(2)}) copy-start(f32[4,4]{1,0:T(4,128)} %copy-done.52) | copy-start | bytes 196
  606.6 30.3 %copy-start.59 = (f32[4,4]{1,0:T(4,128)S(1)}, f32[4,4]{1,0:T(4,128)}, u32[]{:S(2)}) copy-start(f32[4,4]{1,0:T(4,128)} %copy-done.58) | copy-start | bytes 196
  606.6 31.0 %copy-start.55 = (f32[4,4]{1,0:T(4,128)S(1)}, f32[4,4]{1,0:T(4,128)}, u32[]{:S(2)}) copy-start(f32[4,4]{1,0:T(4,128)} %copy-done.54) | copy-start | bytes 196
  606.6 32.6 %copy-start.61 = (f32[4,4]{1,0:T(4,128)S(1)}, f32[4,4]{1,0:T(4,128)}, u32[]{:S(2)}) copy-start(f32[4,4]{1,0:T(4,128)} %copy-done.60) | copy-start | bytes 196
  606.6 32.5 %copy-start.67 = (f32[4,4]{1,0:T(4,128)S(1)}, f32[4,4]{1,0:T(4,128)}, u32[]{:S(2)}) copy-start(f32[4,4]{1,0:T(4,128)} %copy-done.66) | copy-start | bytes 196
  606.6 33.3 %copy-start.63 = (f32[4,4]{1,0:T(4,128)S(1)}, f32[4,4]{1,0:T(4,128)}, u32[]{:S(2)}) copy-start(f32[4,4]{1,0:T(4,128)} %copy-done.62) | copy-start | bytes 196
  606.6 34.8 %copy-start.69 = (f32[4,4]{1,0:T(4,128)S(1)}, f32[4,4]{1,0:T(4,128)}, u32[]{:S(2)}) copy-start(f32[4,4]{1,0:T(4,128)} %copy-done.68) | copy-start | bytes 196
  606.6 35.6 %copy-start.71 = (f32[4,4]{1,0:T(4,128)S(1)}, f32[4,4]{1,0:T(4,128)}, u32[]{:S(2)}) copy-start(f32[4,4]{1,0:T(4,128)} %copy-done.70) | copy-start | bytes 196
  606.6 37.9 %copy-start.43 = (f32[4,4]{1,0:T(4,128)S(1)}, f32[4,4]{1,0:T(4,128)}, u32[]{:S(2)}) copy-start(f32[4,4]{1,0:T(4,128)} %copy-done.42) | copy-start | bytes 196
  606.6 40.3 %copy-start.57 = (f32[4,4]{1,0:T(4,128)S(1)}, f32[4,4]{1,0:T(4,128)}, u32[]{:S(2)}) copy-start(f32[4,4]{1,0:T(4,128)} %copy-done.56) | copy-start | bytes 196
  606.7 42.6 %copy-start.65 = (f32[4,4]{1,0:T(4,128)S(1)}, f32[4,4]{1,0:T(4,128)}, u32[]{:S(2)}) copy-start(f32[4,4]{1,0:T(4,128)} %copy-done.64) | copy-start | bytes 196
  606.7 44.1 %copy-start.20 = (f32[4,4]{1,0:T(4,128)S(1)}, f32[4,4]{1,0:T(4,128)}, u32[]{:S(2)}) copy-start(f32[4,4]{1,0:T(4,128)} %copy-done.19) | copy-start | bytes 196
  (81 other events, 361.7 us)
Sparse Core Ops, SparseCore 0:
  9.6 25.2 all-gather.3
  46.0 99.0 all-gather.5
  610.8 82.2 all-reduce.255
where the time goes:
time: 724 us; the launch traced here: 714 us
  between operations  284 us (39%)
  waiting for transfers between devices  162 us (22%)
  matrix products  108 us (15%)
  local copies, waits for them, and re-layouts  104 us (14%)
  other arithmetic  55 us (8%)
    all_gather x1, waiting for transfers between devices, prefix(): gathered = lax.all_gather(part, axis)  93.8 us
    dot_general x510, matrix products, matmul(): jnp.dot(left, right, precision=lax.Precision.HIGHEST, preferred_element_t...  91.5 us
    slice x128, local copies, waits for them, and re-layouts, factor_inverse(): lower_top, inverse_top = factor_inverse(matrix[:half, :half])  87.6 us
    psum x1, waiting for transfers between devices, spread(): return lax.psum(block, axis)  40.6 us
    concatenate x103, other arithmetic, factor_inverse(): jnp.concatenate([jnp.concatenate([lower_top, upper_zeros], 1), jnp.concat...  39.8 us
    all_gather x1, waiting for transfers between devices, shards(): whole = lax.all_gather(panel_transposed, 'col', axis=0, tiled=True)  26.9 us
  transfers between devices with their start and end apart: 3, of which 3 were waited for; matrix products, arithmetic and copies ran while one was open for 7% of the time, Pallas kernels for 0%

commit v1 on v0

v1 whole, which is shorter than its diff:
```python
import functools

import jax
import jax.numpy as jnp
from jax import lax
from jax.experimental import pallas as pl
from jax.experimental.pallas import tpu as pltpu
from jax.sharding import PartitionSpec as P

F32 = jnp.float32
MESH = pl.DeviceIdType.MESH
BLOCK = 32
GROUP = 4
CHUNKS = 4


def dot(left, right, dims=((1,), (0,))):
    return lax.dot_general(
        left, right, (dims, ((), ())), precision=lax.Precision.HIGHEST, preferred_element_type=F32
    )


def factor_rows(at, width, read, works):
    first = at * BLOCK
    low = (first // 128) * 128
    high = width + min(width, ((first + BLOCK + 127) // 128) * 128)
    spans = list(range(low, high, 128))
    tall = BLOCK // 8
    deep = max(128, ((first + 127) // 128) * 128)
    sub = lax.broadcasted_iota(jnp.int32, (8, 128), 0)
    lane = lax.broadcasted_iota(jnp.int32, (8, 128), 1)
    states = []
    for which, work in enumerate(works):
        update = None
        if at > 0:
            side = work[0:deep, low : low + 128].T[first - low : first - low + BLOCK, :]
            update = dot(side, work[0:deep, low:high])
        rows = []
        for tile in range(tall):
            line = []
            for span in spans:
                row0 = first + tile * 8
                if span < width:
                    value = read(which, row0, span)
                else:
                    value = (sub + row0 == lane + (span - width)).astype(F32)
                if update is not None:
                    value = value - update[tile * 8 : tile * 8 + 8, span - low : span - low + 128]
                line.append(value)
            rows.append(line)
        states.append(rows)
    scales = [[jnp.zeros((8, 128), F32) for _ in range(tall)] for _ in works]
    for start in range(0, BLOCK, GROUP):
        top = start // 8
        spreads = []
        for rows in states:
            spreads.append(
                [
                    {
                        tile: jnp.broadcast_to(
                            rows[tile][0][:, first - low + start + k : first - low + start + k + 1],
                            (8, 128),
                        )
                        for tile in range(top, tall)
                    }
                    for k in range(GROUP)
                ]
            )
        for k in range(GROUP):
            place = (start + k) % 8
            for which, rows in enumerate(states):
                column = spreads[which][k]
                pivot = jnp.broadcast_to(column[top][place : place + 1, :], (8, 128))
                recip = 1.0 / pivot
                scales[which][top] = jnp.where(sub == place, lax.rsqrt(pivot), scales[which][top])
                factors = {tile: column[tile] * recip for tile in range(top, tall)}
                factors[top] = jnp.where(sub > place, factors[top], 0.0)
                for later in range(k + 1, GROUP):
                    other = spreads[which][later]
                    line = jnp.broadcast_to(other[top][place : place + 1, :], (8, 128))
                    for tile in range(top, tall):
                        other[tile] = other[tile] - factors[tile] * line
                for at_span in range(len(spans)):
                    line = jnp.broadcast_to(rows[top][at_span][place : place + 1, :], (8, 128))
                    for tile in range(top, tall):
                        rows[tile][at_span] = rows[tile][at_span] - factors[tile] * line
    for which, work in enumerate(works):
        for tile in range(tall):
            row0 = first + tile * 8
            for at_span, span in enumerate(spans):
                value = states[which][tile][at_span] * scales[which][tile]
                if span < width:
                    value = jnp.where(lane + span >= sub + row0, value, 0.0)
                work[row0 : row0 + 8, span : span + 128] = value


def flip(index, distance):
    return index + distance - 2 * distance * lax.rem(lax.div(index, distance), 2)


def chain_kernel(
    n_row, n_col, panel_ref, trailing_hbm, factors_ref, blocks_ref, coeffs_ref, whole_hbm,
    whole, tv, gsum, gpre, grecv, gfull, csum, cpre, crecv, work_own, work_last,
    local_sem, p_send, p_recv, f_send, f_recv, g_send, g_recv, c_send, c_recv,
    a_send, a_recv, b_send, b_recv,
):
    share, depth = panel_ref.shape
    width = share * n_col
    row, col = lax.axis_index("row"), lax.axis_index("col")
    steps = n_row.bit_length() - 1
    pairs = n_col // 2
    mate = flip(col, 1)
    ahead = [lax.rem(col + 2 * k, n_col) for k in range(1, pairs)]
    behind = [lax.rem(col + n_col - 2 * k, n_col) for k in range(1, pairs)]
    across = [flip(row, 2**h) for h in range(steps)]

    load = pltpu.make_async_copy(trailing_hbm, tv, local_sem.at[0])
    load.start()
    whole[col] = panel_ref[...]

    barrier = pltpu.get_barrier_semaphore()
    for target in [mate] + ahead:
        pl.semaphore_signal(barrier, inc=1, device_id=(row, target), device_id_type=MESH)
    for target in across:
        pl.semaphore_signal(barrier, inc=1, device_id=(target, col), device_id_type=MESH)
    pl.semaphore_wait(barrier, pairs + steps)

    def send(src, dst, send_sem, recv_sem, r, c):
        return pltpu.make_async_remote_copy(
            src_ref=src, dst_ref=dst, send_sem=send_sem, recv_sem=recv_sem,
            device_id=(r, c), device_id_type=MESH,
        )

    piece = depth // CHUNKS
    started = []
    direct = []
    for q in range(CHUNKS):
        cut = pl.ds(q * piece, piece)
        line = []
        for k, target in enumerate(ahead):
            copy = send(panel_ref.at[:, cut], whole.at[col, :, cut], p_send.at[k, q], p_recv.at[k, q], row, target)
            copy.start()
            line.append(copy)
        copy = send(panel_ref.at[:, cut], whole.at[col, :, cut], f_send.at[0, q], f_recv.at[0, q], row, mate)
        copy.start()
        direct.append((line, copy))
    load.wait()
    gram = None
    cross_started = []
    gram_copies = []
    cross_copies = []

    def gram_step(h):
        copy = send(gsum.at[h], grecv.at[h], g_send.at[h], g_recv.at[h], across[h], col)
        copy.start()
        gram_copies.append(copy)

    def gram_take(h):
        gram_copies[h].wait_recv()
        lower = across[h] < row
        gpre[...] = gpre[...] + jnp.where(lower, grecv[h], 0.0)
        gsum[h + 1] = gsum[h] + grecv[h]

    def cross_step(h):
        copy = send(csum.at[h], crecv.at[h], c_send.at[h], c_recv.at[h], across[h], col)
        copy.start()
        cross_copies.append(copy)

    def cross_take(h):
        cross_copies[h].wait_recv()
        lower = across[h] < row
        cpre[...] = cpre[...] + jnp.where(lower, crecv[h], 0.0)
        csum[h + 1] = csum[h] + crecv[h]

    for q in range(CHUNKS):
        cut = pl.ds(q * piece, piece)
        line, near = direct[q]
        forwards = []
        for k, copy in enumerate(line):
            copy.wait_recv()
            on = send(
                whole.at[behind[k], :, cut], whole.at[behind[k], :, cut],
                f_send.at[k + 1, q], f_recv.at[k + 1, q], row, mate,
            )
            on.start()
            forwards.append(on)
            started.append(copy)
        near.wait_recv()
        started.append(near)
        for on in forwards:
            on.wait_recv()
            started.append(on)
        part = whole[:, :, q * piece : (q + 1) * piece].reshape(width, piece)
        own = dot(panel_ref[:, q * piece : (q + 1) * piece], part, ((1,), (1,)))
        gram = own if gram is None else gram + own
        if q == CHUNKS - 1:
            gsum[0] = gram
            gpre[...] = gram
            gram_step(0)
        product = dot(part, tv[q * piece : (q + 1) * piece, :])
        if q == 0:
            csum[0] = product
        else:
            csum[0] = csum[0] + product
    cross_step(0)
    cpre[...] = csum[0]
    out = pltpu.make_async_copy(whole, whole_hbm, local_sem.at[1])
    out.start()
    work_own[...] = jnp.zeros_like(work_own)
    work_last[...] = jnp.zeros_like(work_last)
    for h in range(steps):
        gram_take(h)
        if h + 1 < steps:
            gram_step(h + 1)

    gfull[col, 0] = gpre[...]
    gfull[col, 1] = gsum[steps]
    far = []
    for k, target in enumerate(ahead):
        copy = send(gfull.at[col], gfull.at[col], a_send.at[k], a_recv.at[k], row, target)
        copy.start()
        far.append(copy)
    near = send(gfull.at[col], gfull.at[col], b_send.at[0], b_recv.at[0], row, mate)
    near.start()
    forwards = []
    for k, copy in enumerate(far):
        copy.wait_recv()
        on = send(gfull.at[behind[k]], gfull.at[behind[k]], b_send.at[k + 1], b_recv.at[k + 1], row, mate)
        on.start()
        forwards.append(on)
    near.wait_recv()
    for on in forwards:
        on.wait_recv()

    def read(which, row0, span):
        return gfull[row0 // share, which, row0 % share : row0 % share + 8, span : span + 128]

    count = width // BLOCK
    done = 0
    for at in range(count):
        factor_rows(at, width, read, (work_own, work_last))
        while done < steps and (done + 1) * count <= (at + 1) * steps:
            cross_take(done)
            done += 1
            if done < steps:
                cross_step(done)
    factors_ref[...] = work_own[:, :width]
    middle = dot(work_last[:, width:], csum[steps])
    coeffs_ref[...] = dot(work_last[:, width:], middle, ((0,), (0,)))
    blocks_ref[...] = dot(work_own[:, width:], cpre[...])
    out.wait()
    for copy in started + gram_copies + cross_copies + far + [near] + forwards:
        copy.wait_send()


def chain(panel, trailing, n_row, n_col):
    share, depth = panel.shape
    width = share * n_col
    cols = trailing.shape[1]
    steps = n_row.bit_length() - 1
    pairs = n_col // 2
    dma = pltpu.SemaphoreType.DMA
    vmem = pl.BlockSpec(memory_space=pltpu.VMEM)
    hbm = pl.BlockSpec(memory_space=pl.ANY)
    apart = max(pairs - 1, 1)
    return pl.pallas_call(
        functools.partial(chain_kernel, n_row, n_col),
        out_shape=(
            jax.ShapeDtypeStruct((width, width), F32),
            jax.ShapeDtypeStruct((width, cols), F32),
            jax.ShapeDtypeStruct((width, cols), F32),
            jax.ShapeDtypeStruct((n_col, share, depth), F32),
        ),
        in_specs=[vmem, hbm],
        out_specs=(vmem, vmem, vmem, hbm),
        scratch_shapes=[
            pltpu.VMEM((n_col, share, depth), F32),
            pltpu.VMEM((depth, cols), F32),
            pltpu.VMEM((steps + 1, share, width), F32),
            pltpu.VMEM((share, width), F32),
            pltpu.VMEM((steps, share, width), F32),
            pltpu.VMEM((n_col, 2, share, width), F32),
            pltpu.VMEM((steps + 1, width, cols), F32),
            pltpu.VMEM((width, cols), F32),
            pltpu.VMEM((steps, width, cols), F32),
            pltpu.VMEM((width, 2 * width), F32),
            pltpu.VMEM((width, 2 * width), F32),
            dma((2,)),
            dma((apart, CHUNKS)),
            dma((apart, CHUNKS)),
            dma((pairs, CHUNKS)),
            dma((pairs, CHUNKS)),
            dma((steps,)),
            dma((steps,)),
            dma((steps,)),
            dma((steps,)),
            dma((apart,)),
            dma((apart,)),
            dma((pairs,)),
            dma((pairs,)),
        ],
        compiler_params=pltpu.CompilerParams(
            collective_id=0, has_side_effects=True, vmem_limit_bytes=44 * 2**20
        ),
    )(panel, trailing)


def remove_kernel(whole_ref, coeffs_ref, trailing_ref, out_ref):
    part = whole_ref[...].reshape(coeffs_ref.shape[0], whole_ref.shape[2])
    out_ref[...] = trailing_ref[...] - dot(part, coeffs_ref[...], ((0,), (0,)))


def remove(whole, coeffs, trailing):
    depth, cols = trailing.shape
    n_col, share, _ = whole.shape
    tile = depth // 4
    return pl.pallas_call(
        remove_kernel,
        grid=(depth // tile,),
        out_shape=jax.ShapeDtypeStruct((depth, cols), F32),
        in_specs=[
            pl.BlockSpec((n_col, share, tile), lambda i: (0, 0, i)),
            pl.BlockSpec(coeffs.shape, lambda i: (0, 0)),
            pl.BlockSpec((tile, cols), lambda i: (i, 0)),
        ],
        out_specs=pl.BlockSpec((tile, cols), lambda i: (i, 0)),
        compiler_params=pltpu.CompilerParams(vmem_limit_bytes=32 * 2**20),
    )(whole, coeffs, trailing)


def solution(mesh):
    n_row, n_col = mesh.shape["row"], mesh.shape["col"]

    def shards(panel, trailing):
        factors, blocks, coeffs, whole = chain(panel, trailing, n_row, n_col)
        return factors, blocks, remove(whole, coeffs, trailing)

    return jax.shard_map(
        shards,
        mesh=mesh,
        in_specs=(P("col", "row"), P("row", "col")),
        out_specs=(P("row", None), P("row", "col"), P("row", "col")),
        check_vma=False,
    )
```

time: 724 us -> 94.1 us (0.13); the launches traced: 714 us -> 93.9 us
  between operations: 284 us -> 0.65 us
  waiting for transfers between devices: 162 us -> 0 us
  matrix products: 108 us -> 0 us
  local copies, waits for them, and re-layouts: 104 us -> 4.72 us
  Pallas kernels: 0 us -> 88.5 us
  other arithmetic: 55 us -> 0 us
    all_gather x2 -> x0, waiting for transfers between devices: 121 us -> none  [the longest x1 93.8 us: prefix(): gathered = lax.all_gather(part, axis)]
    dot_general x513 -> x0, matrix products: 108 us -> none  [the longest x510 91.5 us: matmul(): jnp.dot(left, right, precision=lax.Precision.HIGHEST, preferred_element_t...]
    pallas_call x0 -> x2, Pallas kernels: none -> 88.5 us  [the longest x1 83.2 us: chain(): pl.pallas_call(functools.partial(chain_kernel, n_row, n_col), out_shape=(...]
    slice x128 -> x0, local copies, waits for them, and re-layouts: 87.6 us -> none  [factor_inverse(): lower_top, inverse_top = factor_inverse(matrix[:half, :half])]
    concatenate x231 -> x0, other arithmetic: 51.4 us -> none  [the longest x103 39.8 us: factor_inverse(): jnp.concatenate([jnp.concatenate([lower_top, upper_zeros], 1), jnp.concat...]
    psum x1 -> x0, waiting for transfers between devices: 40.6 us -> none  [spread(): return lax.psum(block, axis)]
    unnamed x287 -> x6, local copies, waits for them, and re-layouts: 13.8 us -> 4.72 us
  transfers between devices with their start and end apart: 3 -> 0, of which waited for: 3 -> 0; matrix products, arithmetic and copies ran while one was open for 7% -> 0% of each run, Pallas kernels for 0% -> 0%
where the time goes in v1:
time: 94.1 us; the launch traced here: 93.9 us
  Pallas kernels  88.5 us (94%)
  local copies, waits for them, and re-layouts  4.72 us (5%)
    pallas_call x1, Pallas kernels, chain(): pl.pallas_call(functools.partial(chain_kernel, n_row, n_col), out_shape=(...  83.2 us
    pallas_call x1, Pallas kernels, remove(): pl.pallas_call(remove_kernel, grid=(depth // tile,), out_shape=jax.ShapeD...  5.31 us
    unnamed x6, local copies, waits for them, and re-layouts  4.72 us

profile of v1, /device:TPU:0, one launch (start us, length us, event | category | flops | bytes accessed | tf_op | source)
XLA Modules:
  0.0 93.9 jit_solution(14369063422136712954)
XLA Ops:
  0.6 0.0 copy-start
  0.6 2.2 %copy-done = f32[2048,512]{1,0:T(8,128)S(1)} copy-done((f32[2048,512]{1,0:T(8,128)S(1)}, f32[2048,512]{1,0:T(8,128)}, u32[]{:S(2)}) %copy-start) | copy-done | bytes 4194328
  2.8 0.0 copy-start.1
  2.8 1.0 %copy-done.1 = f32[64,2048]{1,0:T(8,128)S(1)} copy-done((f32[64,2048]{1,0:T(8,128)S(1)}, f32[64,2048]{1,0:T(8,128)}, u32[]{:S(2)}) %copy-start.1) | copy-done | bytes 524312
  3.9 83.2 %shard_map.49 = (f32[256,256]{1,0:T(8,128)S(1)}, f32[256,512]{1,0:T(8,128)S(1)}, f32[256,512]{1,0:T(8,128)S(1)}, f32[4,64,2048]{2,1,0:T(8,128)S(1)}) custom-call(f32[64,2048]{1,0:T(8,128)S(1)} %copy-done.1, f32[2048,512]{1,0:T(8,128)S(1)} %copy-done), custom_call_target="tpu_custom_call" | custom-call | tf_op jit(solution)/shard_map/pallas_call | solution.py:266
  87.1 5.3 %shard_map.50 = f32[2048,512]{1,0:T(8,128)} custom-call(f32[4,64,2048]{2,1,0:T(8,128)S(1)} %get-tuple-element.9.whole_ref, f32[256,512]{1,0:T(8,128)S(1)} %get-tuple-element.10.coeffs_ref, f32[2048,512]{1,0:T(8,128)S(1)} %copy-done), custom_call_target="tpu_custom_call" | custom-call | tf_op jit(solution)/shard_map/pallas_call | solution.py:317
  92.4 0.7 copy.7
  93.1 0.8 copy.8
Async XLA Ops:
  0.6 2.2 %copy-start = (f32[2048,512]{1,0:T(8,128)S(1)}, f32[2048,512]{1,0:T(8,128)}, u32[]{:S(2)}) copy-start(f32[2048,512]{1,0:T(8,128)} %trailing_ref.1) | copy-start | bytes 12582916
  2.8 1.0 %copy-start.1 = (f32[64,2048]{1,0:T(8,128)S(1)}, f32[64,2048]{1,0:T(8,128)}, u32[]{:S(2)}) copy-start(f32[64,2048]{1,0:T(8,128)} %panel_ref.1) | copy-start | bytes 1572868

commit v2 on v1

--- a/solution.py
+++ b/solution.py
@@ -10,7 +10,7 @@
 F32 = jnp.float32
 MESH = pl.DeviceIdType.MESH
 BLOCK = 32
-GROUP = 4
+GROUP = 8
 CHUNKS = 4
 
 
@@ -99,13 +99,14 @@
 
 
 def chain_kernel(
-    n_row, n_col, panel_ref, trailing_hbm, factors_ref, blocks_ref, coeffs_ref, whole_hbm,
-    whole, tv, gsum, gpre, grecv, gfull, csum, cpre, crecv, work_own, work_last,
+    n_row, n_col, panel_hbm, trailing_hbm, factors_ref, blocks_ref, coeffs_ref, whole_hbm,
+    whole, tv, gsum, gpre, grecv, gfull, csum, cpre, crecv, ctotal, cprefix, work_own, work_last,
     local_sem, p_send, p_recv, f_send, f_recv, g_send, g_recv, c_send, c_recv,
     a_send, a_recv, b_send, b_recv,
 ):
-    share, depth = panel_ref.shape
+    share, depth = panel_hbm.shape
     width = share * n_col
+    cols = tv.shape[1]
     row, col = lax.axis_index("row"), lax.axis_index("col")
     steps = n_row.bit_length() - 1
     pairs = n_col // 2
@@ -113,16 +114,22 @@
     ahead = [lax.rem(col + 2 * k, n_col) for k in range(1, pairs)]
     behind = [lax.rem(col + n_col - 2 * k, n_col) for k in range(1, pairs)]
     across = [flip(row, 2**h) for h in range(steps)]
-
+    order = [col, mate]
+    for source in behind:
+        order += [source, flip(source, 1)]
+
+    own_load = pltpu.make_async_copy(panel_hbm, whole.at[col], local_sem.at[2])
+    own_load.start()
     load = pltpu.make_async_copy(trailing_hbm, tv, local_sem.at[0])
     load.start()
-    whole[col] = panel_ref[...]
 
     barrier = pltpu.get_barrier_semaphore()
     for target in [mate] + ahead:
         pl.semaphore_signal(barrier, inc=1, device_id=(row, target), device_id_type=MESH)
     for target in across:
         pl.semaphore_signal(barrier, inc=1, device_id=(target, col), device_id_type=MESH)
+    work_own[...] = jnp.zeros_like(work_own)
+    work_last[...] = jnp.zeros_like(work_last)
     pl.semaphore_wait(barrier, pairs + steps)
 
     def send(src, dst, send_sem, recv_sem, r, c):
@@ -132,23 +139,22 @@
         )
 
     piece = depth // CHUNKS
+    own_load.wait()
     started = []
     direct = []
     for q in range(CHUNKS):
         cut = pl.ds(q * piece, piece)
         line = []
         for k, target in enumerate(ahead):
-            copy = send(panel_ref.at[:, cut], whole.at[col, :, cut], p_send.at[k, q], p_recv.at[k, q], row, target)
+            copy = send(whole.at[col, :, cut], whole.at[col, :, cut], p_send.at[k, q], p_recv.at[k, q], row, target)
             copy.start()
             line.append(copy)
-        copy = send(panel_ref.at[:, cut], whole.at[col, :, cut], f_send.at[0, q], f_recv.at[0, q], row, mate)
+        copy = send(whole.at[col, :, cut], whole.at[col, :, cut], f_send.at[0, q], f_recv.at[0, q], row, mate)
         copy.start()
         direct.append((line, copy))
-    load.wait()
     gram = None
-    cross_started = []
     gram_copies = []
-    cross_copies = []
+    cross_copies = {}
 
     def gram_step(h):
         copy = send(gsum.at[h], grecv.at[h], g_send.at[h], g_recv.at[h], across[h], col)
@@ -161,22 +167,42 @@
         gpre[...] = gpre[...] + jnp.where(lower, grecv[h], 0.0)
         gsum[h + 1] = gsum[h] + grecv[h]
 
-    def cross_step(h):
-        copy = send(csum.at[h], crecv.at[h], c_send.at[h], c_recv.at[h], across[h], col)
+    def cross_step(at, h):
+        copy = send(csum.at[h, at], crecv.at[h, at], c_send.at[h, at], c_recv.at[h, at], across[h], col)
         copy.start()
-        cross_copies.append(copy)
-
-    def cross_take(h):
-        cross_copies[h].wait_recv()
+        cross_copies[at, h] = copy
+
+    def cross_take(at, h):
+        cross_copies[at, h].wait_recv()
         lower = across[h] < row
-        cpre[...] = cpre[...] + jnp.where(lower, crecv[h], 0.0)
-        csum[h + 1] = csum[h] + crecv[h]
-
+        before = cpre[at] + jnp.where(lower, crecv[h, at], 0.0)
+        total = csum[h, at] + crecv[h, at]
+        if h + 1 < steps:
+            cpre[at] = before
+            csum[h + 1, at] = total
+            cross_step(at, h + 1)
+        else:
+            cprefix[order[at]] = before
+            ctotal[order[at]] = total
+
+    def cross_start(pair):
+        slices = [whole[order[2 * pair]], whole[order[2 * pair + 1]]]
+        both = dot(jnp.concatenate(slices, 0), tv[...])
+        for half, at in enumerate((2 * pair, 2 * pair + 1)):
+            own = both[half * share : (half + 1) * share]
+            csum[0, at] = own
+            cpre[at] = own
+            cross_step(at, 0)
+
+    load.wait()
+    for _, near in direct:
+        near.wait_recv()
+        started.append(near)
+    cross_start(0)
     for q in range(CHUNKS):
         cut = pl.ds(q * piece, piece)
-        line, near = direct[q]
         forwards = []
-        for k, copy in enumerate(line):
+        for k, copy in enumerate(direct[q][0]):
             copy.wait_recv()
             on = send(
                 whole.at[behind[k], :, cut], whole.at[behind[k], :, cut],
@@ -185,29 +211,22 @@
             on.start()
             forwards.append(on)
             started.append(copy)
-        near.wait_recv()
-        started.append(near)
+        if q == 1:
+            cross_take(0, 0)
+            cross_take(1, 0)
         for on in forwards:
             on.wait_recv()
             started.append(on)
         part = whole[:, :, q * piece : (q + 1) * piece].reshape(width, piece)
-        own = dot(panel_ref[:, q * piece : (q + 1) * piece], part, ((1,), (1,)))
+        own = dot(whole[col, :, q * piece : (q + 1) * piece], part, ((1,), (1,)))
         gram = own if gram is None else gram + own
-        if q == CHUNKS - 1:
-            gsum[0] = gram
-            gpre[...] = gram
-            gram_step(0)
-        product = dot(part, tv[q * piece : (q + 1) * piece, :])
-        if q == 0:
-            csum[0] = product
-        else:
-            csum[0] = csum[0] + product
-    cross_step(0)
-    cpre[...] = csum[0]
+    gsum[0] = gram
+    gpre[...] = gram
+    gram_step(0)
     out = pltpu.make_async_copy(whole, whole_hbm, local_sem.at[1])
     out.start()
-    work_own[...] = jnp.zeros_like(work_own)
-    work_last[...] = jnp.zeros_like(work_last)
+    for pair in range(1, pairs):
+        cross_start(pair)
     for h in range(steps):
         gram_take(h)
         if h + 1 < steps:
@@ -222,6 +241,13 @@
         far.append(copy)
     near = send(gfull.at[col], gfull.at[col], b_send.at[0], b_recv.at[0], row, mate)
     near.start()
+    pending = [(at, h) for h in range(1, steps) for at in (0, 1)]
+    late = [(at, h) for h in range(steps) for at in range(2, n_col)]
+    if steps > 1:
+        for at in (0, 1):
+            cross_take(*pending.pop(0))
+    for _ in range(n_col - 2):
+        cross_take(*late.pop(0))
     forwards = []
     for k, copy in enumerate(far):
         copy.wait_recv()
@@ -236,20 +262,18 @@
         return gfull[row0 // share, which, row0 % share : row0 % share + 8, span : span + 128]
 
     count = width // BLOCK
-    done = 0
+    rest = sorted(pending + late, key=lambda turn: (turn[1], turn[0]))
+    held = len(rest)
     for at in range(count):
         factor_rows(at, width, read, (work_own, work_last))
-        while done < steps and (done + 1) * count <= (at + 1) * steps:
-            cross_take(done)
-            done += 1
-            if done < steps:
-                cross_step(done)
+        while rest and (held - len(rest) + 1) * count <= (at + 1) * held:
+            cross_take(*rest.pop(0))
     factors_ref[...] = work_own[:, :width]
-    middle = dot(work_last[:, width:], csum[steps])
+    middle = dot(work_last[:, width:], ctotal[...].reshape(width, cols))
     coeffs_ref[...] = dot(work_last[:, width:], middle, ((0,), (0,)))
-    blocks_ref[...] = dot(work_own[:, width:], cpre[...])
+    blocks_ref[...] = dot(work_own[:, width:], cprefix[...].reshape(width, cols))
     out.wait()
-    for copy in started + gram_copies + cross_copies + far + [near] + forwards:
+    for copy in started + gram_copies + list(cross_copies.values()) + far + [near] + forwards:
         copy.wait_send()
 
 
@@ -271,7 +295,7 @@
             jax.ShapeDtypeStruct((width, cols), F32),
             jax.ShapeDtypeStruct((n_col, share, depth), F32),
         ),
-        in_specs=[vmem, hbm],
+        in_specs=[hbm, hbm],
         out_specs=(vmem, vmem, vmem, hbm),
         scratch_shapes=[
             pltpu.VMEM((n_col, share, depth), F32),
@@ -280,27 +304,29 @@
             pltpu.VMEM((share, width), F32),
             pltpu.VMEM((steps, share, width), F32),
             pltpu.VMEM((n_col, 2, share, width), F32),
-            pltpu.VMEM((steps + 1, width, cols), F32),
-            pltpu.VMEM((width, cols), F32),
-            pltpu.VMEM((steps, width, cols), F32),
+            pltpu.VMEM((steps, n_col, share, cols), F32),
+            pltpu.VMEM((n_col, share, cols), F32),
+            pltpu.VMEM((steps, n_col, share, cols), F32),
+            pltpu.VMEM((n_col, share, cols), F32),
+            pltpu.VMEM((n_col, share, cols), F32),
             pltpu.VMEM((width, 2 * width), F32),
             pltpu.VMEM((width, 2 * width), F32),
-            dma((2,)),
+            dma((3,)),
             dma((apart, CHUNKS)),
             dma((apart, CHUNKS)),
             dma((pairs, CHUNKS)),
             dma((pairs, CHUNKS)),
             dma((steps,)),
             dma((steps,)),
-            dma((steps,)),
-            dma((steps,)),
+            dma((steps, n_col)),
+            dma((steps, n_col)),
             dma((apart,)),
             dma((apart,)),
             dma((pairs,)),
             dma((pairs,)),
         ],
         compiler_params=pltpu.CompilerParams(
-            collective_id=0, has_side_effects=True, vmem_limit_bytes=44 * 2**20
+            collective_id=0, has_side_effects=True, vmem_limit_bytes=56 * 2**20
         ),
     )(panel, trailing)
 
@@ -324,7 +350,7 @@
             pl.BlockSpec((tile, cols), lambda i: (i, 0)),
         ],
         out_specs=pl.BlockSpec((tile, cols), lambda i: (i, 0)),
-        compiler_params=pltpu.CompilerParams(vmem_limit_bytes=32 * 2**20),
+        compiler_params=pltpu.CompilerParams(vmem_limit_bytes=56 * 2**20),
     )(whole, coeffs, trailing)
 
 

time: 94.1 us -> 69.6 us (0.74)
  Pallas kernels: 88.5 us -> 67.2 us
  local copies, waits for them, and re-layouts: 4.72 us -> 1.5 us
    pallas_call x1, Pallas kernels: 83.2 us -> 59.5 us  [chain(): pl.pallas_call(functools.partial(chain_kernel, n_row, n_col), out_shape=(...]
    unnamed x6, local copies, waits for them, and re-layouts: 4.72 us -> 1.5 us
    pallas_call x1, Pallas kernels: 5.31 us -> 7.74 us  [remove(): pl.pallas_call(remove_kernel, grid=(depth // tile,), out_shape=jax.ShapeD...]
where the time goes in v2:
time: 69.6 us; the launch traced here: 69.4 us
  Pallas kernels  67.2 us (97%)
  local copies, waits for them, and re-layouts  1.5 us (2%)
    pallas_call x1, Pallas kernels, chain(): pl.pallas_call(functools.partial(chain_kernel, n_row, n_col), out_shape=(...  59.5 us
    pallas_call x1, Pallas kernels, remove(): pl.pallas_call(remove_kernel, grid=(depth // tile,), out_shape=jax.ShapeD...  7.74 us
    unnamed x6, local copies, waits for them, and re-layouts  1.5 us

profile of v2, /device:TPU:0, one launch (start us, length us, event | category | flops | bytes accessed | tf_op | source)
XLA Modules:
  0.0 69.4 jit_solution(16687948080977092899)
XLA Ops:
  0.6 59.5 %shard_map.49 = (f32[256,256]{1,0:T(8,128)}, f32[256,512]{1,0:T(8,128)}, f32[256,512]{1,0:T(8,128)}, f32[4,64,2048]{2,1,0:T(8,128)}) custom-call(f32[64,2048]{1,0:T(8,128)} %panel_hbm.1, f32[2048,512]{1,0:T(8,128)} %trailing_ref.1), custom_call_target="tpu_custom_call" | custom-call | tf_op jit(solution)/shard_map/pallas_call | solution.py:290
  60.1 0.0 copy-start.1
  60.2 0.0 copy-start
  60.2 7.7 %shard_map.50 = f32[2048,512]{1,0:T(8,128)} custom-call(f32[4,64,2048]{2,1,0:T(8,128)} %get-tuple-element.9.whole_ref, f32[256,512]{1,0:T(8,128)} %get-tuple-element.10.coeffs_ref, f32[2048,512]{1,0:T(8,128)} %trailing_ref.1), custom_call_target="tpu_custom_call" | custom-call | tf_op jit(solution)/shard_map/pallas_call | solution.py:343
  67.9 0.0 copy-done.1
  67.9 0.7 %copy.7 = f32[256,256]{1,0:T(8,128)} copy(f32[256,256]{1,0:T(8,128)S(1)} %copy-done.1) | data formatting | bytes 524288
  68.6 0.0 copy-done
  68.6 0.8 %copy.8 = f32[256,512]{1,0:T(8,128)} copy(f32[256,512]{1,0:T(8,128)S(1)} %copy-done) | data formatting | bytes 1048576
Async XLA Ops:
  60.1 7.8 %copy-start.1 = (f32[256,256]{1,0:T(8,128)S(1)}, f32[256,256]{1,0:T(8,128)}, u32[]{:S(2)}) copy-start(f32[256,256]{1,0:T(8,128)} %get-tuple-element.14) | copy-start | bytes 786436
  60.2 8.5 %copy-start = (f32[256,512]{1,0:T(8,128)S(1)}, f32[256,512]{1,0:T(8,128)}, u32[]{:S(2)}) copy-start(f32[256,512]{1,0:T(8,128)} %get-tuple-element.15) | copy-start | bytes 1572868
